TPU v7x, 32 devices: a whole 2x2x4 slice. The times are simulated.
32 devices in a mesh: replica: 2 (over y), mp: 16 (over z, x, core).
Axes of the slice: x: 2, y: 2, z: 4, core: 2. Of those that a mesh axis runs over, the one named last changes fastest.
Arguments:
- owner_shard: int32 [64, 256], P(('replica', 'mp')), may hold values from 0 to 15, as said below
- slot_index: int32 [64, 256], P(('replica', 'mp')), may hold values from 0 to 127
- lengths: int32 [64], P(('replica', 'mp')), may hold values from 32 to 256
- labels: float32 [64, 256], P(('replica', 'mp')), may hold values from 0 to 1
- embed_table: bfloat16 [32768, 256], P('mp'), may hold values from -3 to 3
- accumulator: float32 [32768], P('mp'), may hold values from 0.1 to 10
- touched: int32 [2048], P('mp'), may hold values from 0 to 2047, as said below
- w_in: bfloat16 [256, 1024], replicated, may hold values from -0.375 to 0.375
- w_mid: bfloat16 [1024, 1024], replicated, may hold values from -0.1875 to 0.1875
- norm_gain: float32 [1024], replicated, may hold values from 0.5 to 2
- w_out: float32 [1024], replicated, may hold values from -0.1875 to 0.1875
Outputs:
- table_out: bfloat16 [32768, 256], P('mp')
- accum_out: float32 [32768], P('mp')
Inputs may be any that keep to these rules, and one draw needn't show every extreme that they name: `owner_shard`: among the events of one device, every shard is named at most 64 times, and one shard, the same for all devices, is named exactly 64 times by every device. `touched`: the 128 entries of each shard are distinct rows of that shard.
All inputs are finite; a program needn't handle non-finite values.
Results may differ from a plain program's by a relative error of at most 0.0034.
Values may be sent and summed in bfloat16 or wider, within the bound.
No kernel may reach another device: no remote copies, remote signals or barrier semaphores. Data moves between devices by JAX's collectives and lax.ppermute only.
A program may use at most 64 MiB of HBM per device.

v0:
```python
import functools

import jax
import jax.numpy as jnp
from jax import lax
from jax.experimental import pallas as pl
from jax.experimental.pallas import tpu as pltpu
from jax.sharding import PartitionSpec as P


learn_rate = 1.0
F32 = jnp.float32
BF16 = jnp.bfloat16
WHOLE = pl.BlockSpec(memory_space=pltpu.VMEM)
IN_HBM = pl.BlockSpec(memory_space=pltpu.HBM)


def split3(values):
    high = values.astype(BF16)
    rest = values - high.astype(F32)
    middle = rest.astype(BF16)
    low = (rest - middle.astype(F32)).astype(BF16)
    return high, middle, low


def dot_rows(left, right):
    return lax.dot_general(left, right, (((1,), (1,)), ((), ())), preferred_element_type=F32)


def eye(size):
    return lax.broadcasted_iota(jnp.int32, (size, size), 0) == lax.broadcasted_iota(
        jnp.int32, (size, size), 1
    )


def to_column(row):
    size = row.shape[1]
    return jnp.sum(jnp.where(eye(size), row, jnp.zeros_like(row)), axis=1, keepdims=True)


def to_row(column):
    size = column.shape[0]
    return jnp.sum(jnp.where(eye(size), column, jnp.zeros_like(column)), axis=0, keepdims=True)


def event_sums_kernel(shards, lengths_ref, owner_ref, slot_ref, label_ref, out_ref):
    samples, length = owner_ref.shape
    touch = out_ref.shape[2] // 2
    total = jnp.zeros((4 * shards, touch), F32)
    for s in range(samples):
        place = lax.broadcasted_iota(jnp.int32, (shards, length), 1)
        shard = lax.broadcasted_iota(jnp.int32, (shards, length), 0)
        chosen = (owner_ref[s : s + 1, :] == shard) & (place < lengths_ref[:, s : s + 1])
        slot = lax.broadcasted_iota(jnp.int32, (touch, length), 0)
        slots = jnp.where(slot_ref[s : s + 1, :] == slot, 1.0, 0.0).astype(BF16)
        labels = jnp.where(chosen, label_ref[s : s + 1, :], 0.0)
        left = jnp.concatenate([jnp.where(chosen, 1.0, 0.0).astype(BF16), *split3(labels)], axis=0)
        total = total + dot_rows(left, slots)
    count = total[:shards]
    label_sum = total[shards : 2 * shards] + total[2 * shards : 3 * shards] + total[3 * shards :]
    for r in range(out_ref.shape[0] // shards):
        out_ref[r * shards : (r + 1) * shards, 0, :touch] = count
        out_ref[r * shards : (r + 1) * shards, 0, touch:] = label_sum


def row_gradients_kernel(
    touched_hbm,
    table_hbm,
    acc_hbm,
    w_in_hbm,
    w_mid_hbm,
    gain_hbm,
    w_out_hbm,
    table_ref,
    spread_ref,
    old_ref,
    grad_ref,
    stats_ref,
    acc_ref,
    touched_ref,
    w_in_ref,
    w_mid_ref,
    gain_ref,
    w_out_ref,
    sems,
):
    copies = [
        pltpu.make_async_copy(source, target, sems.at[i])
        for i, (source, target) in enumerate(
            (
                (touched_hbm, touched_ref),
                (table_hbm, table_ref),
                (w_in_hbm, w_in_ref),
                (gain_hbm, gain_ref),
                (w_mid_hbm, w_mid_ref),
                (w_out_hbm, w_out_ref),
                (acc_hbm, acc_ref),
            )
        )
    ]
    for copy in copies:
        copy.start()
    touched_copy, table_copy, w_in_copy, gain_copy, w_mid_copy, w_out_copy, acc_copy = copies

    rows = table_ref.shape[0]
    touched_copy.wait()
    touched = touched_ref[...]
    touch = touched.shape[1]
    picks = jnp.where(
        lax.broadcasted_iota(jnp.int32, (touch, rows), 1) == to_column(touched), 1.0, 0.0
    ).astype(BF16)
    table_copy.wait()
    old = jnp.dot(picks, table_ref[...], preferred_element_type=F32).astype(BF16)
    old_ref[...] = old

    w_in_copy.wait()
    pre = jnp.dot(old, w_in_ref[...], preferred_element_type=F32)
    sig_pre = jax.nn.sigmoid(pre)
    hidden = pre * sig_pre
    inv_rms = lax.rsqrt(jnp.mean(hidden * hidden, axis=-1, keepdims=True) + 1e-06)
    gain_copy.wait()
    gain = gain_ref[...]
    normed = (hidden * inv_rms * gain).astype(BF16)
    w_mid_copy.wait()
    mixed = jnp.dot(normed, w_mid_ref[...], preferred_element_type=F32)
    sig_mixed = jax.nn.sigmoid(mixed)
    output = hidden + mixed * sig_mixed
    w_out_copy.wait()
    w_out = w_out_ref[...]
    logits = jnp.sum(output * w_out, axis=-1, keepdims=True)
    d_mixed = (w_out * (sig_mixed * (1.0 + mixed * (1.0 - sig_mixed)))).astype(BF16)
    gained = dot_rows(d_mixed, w_mid_ref[...]) * gain
    d_hidden = (
        w_out
        + inv_rms * gained
        - hidden * inv_rms**3 * jnp.mean(hidden * gained, axis=-1, keepdims=True)
    )
    d_pre = (d_hidden * (sig_pre * (1.0 + pre * (1.0 - sig_pre)))).astype(BF16)
    grad = dot_rows(d_pre, w_in_ref[...])
    grad_ref[...] = grad

    acc_copy.wait()
    acc = acc_ref[...]
    blocks, lanes = acc.shape
    in_lane = lax.broadcasted_iota(jnp.int32, (lanes, touch), 0) == touched % lanes
    in_block = lax.broadcasted_iota(jnp.int32, (blocks, touch), 0) == touched // lanes
    lane_pick = jnp.where(in_lane, 1.0, 0.0).astype(BF16)
    found = sum(jnp.dot(part, lane_pick, preferred_element_type=F32) for part in split3(acc))
    stats_ref[0:1, :] = to_row(logits)
    stats_ref[1:2, :] = to_row(jnp.sum(grad * grad, axis=-1, keepdims=True))
    stats_ref[2:3, :] = jnp.sum(jnp.where(in_block, found, 0.0), axis=0, keepdims=True)
    stats_ref[3:4, :] = touched.astype(F32)

    step = min(rows, 256)
    for start in range(0, rows, step):
        spread = jnp.where(
            lax.broadcasted_iota(jnp.int32, (step, touch), 0) + start == touched, 1.0, 0.0
        )
        spread_ref[start : start + step, :] = spread.astype(BF16)
        kept = jnp.sum(spread, axis=1, keepdims=True) == 0.0
        part = table_ref[start : start + step, :]
        table_ref[start : start + step, :] = jnp.where(kept, part.astype(F32), 0.0).astype(BF16)


def row_update_kernel(
    got_ref, stats_ref, acc_ref, old_ref, grad_ref, spread_ref, base_ref, table_hbm, acc_hbm,
    new_ref, new_acc_ref, sems,
):
    rows, touch = spread_ref.shape
    step = new_ref.shape[1]
    parts = rows // step
    summed = jnp.sum(got_ref[...], axis=0)
    logits = stats_ref[0:1, :]
    d_logit = jax.nn.sigmoid(logits) * summed[:, :touch] - summed[:, touch:]
    acc_new = stats_ref[2:3, :] + d_logit * d_logit * stats_ref[1:2, :]

    factor = to_column(learn_rate * d_logit * lax.rsqrt(acc_new))
    new_rows = (old_ref[...].astype(F32) - factor * grad_ref[...]).astype(BF16)
    copies = []
    for part in range(parts):
        start = part * step
        moved = jnp.dot(
            spread_ref[start : start + step, :], new_rows, preferred_element_type=F32
        )
        new_ref[part] = base_ref[start : start + step, :] + moved.astype(BF16)
        copy = pltpu.make_async_copy(
            new_ref.at[part], table_hbm.at[pl.ds(start, step), :], sems.at[part]
        )
        copy.start()
        copies.append(copy)

    touched = stats_ref[3:4, :].astype(jnp.int32)
    acc = acc_ref[...]
    blocks, lanes = acc.shape
    in_lane = lax.broadcasted_iota(jnp.int32, (lanes, touch), 0) == touched % lanes
    in_block = lax.broadcasted_iota(jnp.int32, (blocks, touch), 0) == touched // lanes
    lane_pick = jnp.where(in_lane, 1.0, 0.0).astype(BF16)
    block_pick = jnp.where(in_block, 1.0, 0.0).astype(BF16)
    left = jnp.concatenate([block_pick, *split3(jnp.where(in_block, acc_new, 0.0))], axis=0)
    placed = dot_rows(left, lane_pick)
    written = placed[blocks : 2 * blocks] + placed[2 * blocks : 3 * blocks] + placed[3 * blocks :]
    new_acc_ref[...] = jnp.where(placed[:blocks] > 0.5, written, acc)
    copy = pltpu.make_async_copy(new_acc_ref, acc_hbm, sems.at[parts])
    copy.start()
    copies.append(copy)
    for copy in copies:
        copy.wait()


def on_device(
    owner_shard,
    slot_index,
    lengths,
    labels,
    embed_table,
    accumulator,
    touched,
    w_in,
    w_mid,
    norm_gain,
    w_out,
):
    shards = lax.axis_size("mp")
    replicas = lax.axis_size("replica")
    rows, width = embed_table.shape
    touch = touched.shape[0]
    lanes = 128

    def stay(array):
        return pltpu.with_memory_space_constraint(array, pltpu.HBM)

    sums = pl.pallas_call(
        functools.partial(event_sums_kernel, shards),
        out_shape=pltpu.VMEM((replicas * shards, 1, 2 * touch), F32),
        in_specs=[WHOLE] * 4,
        out_specs=WHOLE,
        name="event_sums",
    )(stay(lengths.reshape(1, -1)), stay(owner_shard), stay(slot_index), stay(labels))
    got = lax.all_to_all(sums, ("replica", "mp"), 0, 0, tiled=True)

    acc = accumulator.reshape(rows // lanes, lanes)
    gain_row = norm_gain.reshape(1, -1)
    w_out_row = w_out.reshape(1, -1)
    touched_row = touched.reshape(1, touch)
    base, spread, old, grad, stats, acc_copy = pl.pallas_call(
        row_gradients_kernel,
        out_shape=(
            pltpu.VMEM((rows, width), BF16),
            pltpu.VMEM((rows, touch), BF16),
            pltpu.VMEM((touch, width), BF16),
            pltpu.VMEM((touch, width), F32),
            pltpu.VMEM((8, touch), F32),
            pltpu.VMEM(acc.shape, F32),
        ),
        in_specs=[IN_HBM] * 7,
        out_specs=(WHOLE,) * 6,
        scratch_shapes=[
            pltpu.VMEM(touched_row.shape, jnp.int32),
            pltpu.VMEM(w_in.shape, BF16),
            pltpu.VMEM(w_mid.shape, BF16),
            pltpu.VMEM(gain_row.shape, F32),
            pltpu.VMEM(w_out_row.shape, F32),
            pltpu.SemaphoreType.DMA((7,)),
        ],
        compiler_params=pltpu.CompilerParams(vmem_limit_bytes=24 * 1024 * 1024),
        cost_estimate=pl.CostEstimate(
            flops=1_000_000_000, bytes_accessed=5_000_000, transcendentals=300_000
        ),
        name="row_gradients",
    )(
        stay(touched_row),
        stay(embed_table),
        stay(acc),
        stay(w_in),
        stay(w_mid),
        stay(gain_row),
        stay(w_out_row),
    )

    step = min(rows, 512)
    table_out, acc_out = pl.pallas_call(
        row_update_kernel,
        out_shape=(
            pltpu.HBM((rows, width), BF16),
            pltpu.HBM(acc.shape, F32),
        ),
        in_specs=[WHOLE] * 7,
        out_specs=(IN_HBM, IN_HBM),
        scratch_shapes=[
            pltpu.VMEM((rows // step, step, width), BF16),
            pltpu.VMEM(acc.shape, F32),
            pltpu.SemaphoreType.DMA((rows // step + 1,)),
        ],
        compiler_params=pltpu.CompilerParams(vmem_limit_bytes=16 * 1024 * 1024),
        name="row_update",
    )(got, stats, acc_copy, old, grad, spread, base)
    return (table_out, acc_out.reshape(rows))


def solution(mesh):
    in_specs = (
        P(("replica", "mp"), None),
        P(("replica", "mp"), None),
        P(("replica", "mp")),
        P(("replica", "mp"), None),
        P("mp", None),
        P("mp"),
        P("mp"),
        P(),
        P(),
        P(),
        P(),
    )
    out_specs = (P("mp", None), P("mp"))
    return jax.shard_map(
        on_device, mesh=mesh, in_specs=in_specs, out_specs=out_specs, check_vma=False
    )
```

profile of v0, /device:TPU:0, one launch (start us, length us, event | category | flops | bytes accessed | tf_op | source)
XLA Modules:
  0.0 18.2 jit_solution(9260426508708676972)
XLA Ops:
  0.6 1.6 %event_sums.1 = f32[32,1,256]{2,1,0:T(1,128)} custom-call(s32[1,2]{1,0:T(1,128)} %bitcast.6, s32[2,256]{1,0:T(2,128)} %owner_ref.1, s32[2,256]{1,0:T(2,128)} %slot_ref.1, f32[2,256]{1,0:T(2,128)} %label_ref.1), custom_call_target="tpu_custom_call" | custom-call | tf_op jit(solution)/shard_map/event_sums/pallas_call | solution.py:232
  2.2 7.3 %all-to-all-start = ((f32[32,1,256]{2,1,0:T(1,128)}), f32[32,1,256]{2,1,0:T(1,128)S(1)}, u32[]{:S(2)}, u32[]{:S(2)}) async-start(f32[32,1,256]{2,1,0:T(1,128)} %event_sums.1), calls=%async_computation | async-start | bytes 65536 | tf_op jit(solution)/shard_map/all_to_all | solution.py:239
  9.5 4.4 %row_gradients.1 = (bf16[2048,256]{1,0:T(8,128)(2,1)S(1)}, bf16[2048,128]{1,0:T(8,128)(2,1)S(1)}, bf16[128,256]{1,0:T(8,128)(2,1)S(1)}, f32[128,256]{1,0:T(8,128...) custom-call(s32[1,128]{1,0:T(1,128)} %bitcast.11, bf16[2048,256]{1,0:T(8,128)(2,1)} %table_hbm.1, f32[16,128]{1,0:T(8,128)} %bitcast.7, ...), custom_call_target="tpu_custom_call" | custom-call | flops 1000000000 | bytes 5000000 | tf_op jit(solution)/shard_map/row_gradients/pallas_call | solution.py:245
  13.9 2.9 %all-to-all-done.got_ref = f32[32,1,256]{2,1,0:T(1,128)S(1)} async-done(((f32[32,1,256]{2,1,0:T(1,128)}), f32[32,1,256]{2,1,0:T(1,128)S(1)}, u32[]{:S(2)}, u32[]{:S(2)}) %all-to-all-start) | async-done | bytes 32800 | tf_op jit(solution)/shard_map/all_to_all | solution.py:239
  16.8 1.4 %row_update.1 = (bf16[2048,256]{1,0:T(8,128)(2,1)}, f32[16,128]{1,0:T(8,128)}) custom-call(f32[32,1,256]{2,1,0:T(1,128)S(1)} %all-to-all-done.got_ref, f32[8,128]{1,0:T(8,128)S(1)} %get-tuple-element.10.stats_ref, f32[16,128]{1,0:T(8,128)S(1)} %get-tuple-element.11.acc_ref, bf16[128,256]{1,0:T(8,128)(2,1)S(1)} %get-tuple-element.12.old_ref, ...), custom_call_target="tpu_custom_call" | custom-call | tf_op jit(solution)/shard_map/row_update/pallas_call | solution.py:281
Async XLA Ops:
  2.2 14.6 %all-to-all-start = ((f32[32,1,256]{2,1,0:T(1,128)}), f32[32,1,256]{2,1,0:T(1,128)S(1)}, u32[]{:S(2)}, u32[]{:S(2)}) async-start(f32[32,1,256]{2,1,0:T(1,128)} %event_sums.1), calls=%async_computation | async-start | bytes 65536 | tf_op jit(solution)/shard_map/all_to_all | solution.py:239
where the time goes:
time: 18.4 us; the launch traced here: 18.2 us
  Pallas kernels  7.36 us (40%)
  starting transfers between devices  7.3 us (40%)
  waiting for transfers between devices  2.88 us (16%)
  between operations  0.65 us (4%)
    all_to_all x1, starting transfers between devices, on_device(): got = lax.all_to_all(sums, ('replica', 'mp'), 0, 0, tiled=True)  7.3 us
    pallas_call x1, Pallas kernels, on_device(): pl.pallas_call(row_gradients_kernel, out_shape=(pltpu.VMEM((rows, width),...  4.36 us
    all_to_all x1, waiting for transfers between devices, on_device(): got = lax.all_to_all(sums, ('replica', 'mp'), 0, 0, tiled=True)  2.88 us
    pallas_call x1, Pallas kernels, on_device(): pl.pallas_call(functools.partial(event_sums_kernel, shards), out_shape=pl...  1.57 us
    pallas_call x1, Pallas kernels, on_device(): pl.pallas_call(row_update_kernel, out_shape=(pltpu.HBM((rows, width), BF1...  1.43 us
  transfers between devices with their start and end apart: 1, of which 1 were waited for; matrix products, arithmetic and copies ran while one was open for 0% of the time, Pallas kernels for 24%

commit v1 on v0

v1 whole, which is shorter than its diff:
```python
import functools

import jax
import jax.numpy as jnp
from jax import lax
from jax.experimental import pallas as pl
from jax.experimental.pallas import tpu as pltpu
from jax.sharding import PartitionSpec as P


learn_rate = 1.0
F32 = jnp.float32
BF16 = jnp.bfloat16
WHOLE = pl.BlockSpec(memory_space=pltpu.VMEM)
IN_HBM = pl.BlockSpec(memory_space=pltpu.HBM)


def split3(values):
    high = values.astype(BF16)
    rest = values - high.astype(F32)
    middle = rest.astype(BF16)
    low = (rest - middle.astype(F32)).astype(BF16)
    return high, middle, low


def dot_rows(left, right):
    return lax.dot_general(left, right, (((1,), (1,)), ((), ())), preferred_element_type=F32)


def eye(size):
    return lax.broadcasted_iota(jnp.int32, (size, size), 0) == lax.broadcasted_iota(
        jnp.int32, (size, size), 1
    )


def to_column(row):
    size = row.shape[1]
    return jnp.sum(jnp.where(eye(size), row, jnp.zeros_like(row)), axis=1, keepdims=True)


def to_row(column):
    size = column.shape[0]
    return jnp.sum(jnp.where(eye(size), column, jnp.zeros_like(column)), axis=0, keepdims=True)


def copies_of(pairs, sems):
    return [
        pltpu.make_async_copy(source, target, sems.at[i]) for i, (source, target) in enumerate(pairs)
    ]


def start_all(copies):
    for copy in copies:
        copy.start()


def place_in_mesh():
    replica, place = lax.axis_index("replica"), lax.axis_index("mp")
    replicas, places = lax.axis_size("replica"), lax.axis_size("mp")
    steps = replica + place // 4 + (place // 2) % 2
    most = replicas - 1 + (places - 1) // 4 + 1
    near = 5 * steps < 2 * most
    middle = jnp.logical_and(jnp.logical_not(near), 2 * steps < most)
    return near, middle


def event_sums(lengths_ref, owner_ref, slot_ref, label_ref, out_ref, shards):
    samples, length = owner_ref.shape
    touch = out_ref.shape[2] // 2
    total = jnp.zeros((4 * shards, touch), F32)
    for s in range(samples):
        place = lax.broadcasted_iota(jnp.int32, (shards, length), 1)
        shard = lax.broadcasted_iota(jnp.int32, (shards, length), 0)
        chosen = (owner_ref[s : s + 1, :] == shard) & (place < lengths_ref[:, s : s + 1])
        slot = lax.broadcasted_iota(jnp.int32, (touch, length), 0)
        slots = jnp.where(slot_ref[s : s + 1, :] == slot, 1.0, 0.0).astype(BF16)
        labels = jnp.where(chosen, label_ref[s : s + 1, :], 0.0)
        left = jnp.concatenate([jnp.where(chosen, 1.0, 0.0).astype(BF16), *split3(labels)], axis=0)
        total = total + dot_rows(left, slots)
    count = total[:shards]
    label_sum = total[shards : 2 * shards] + total[2 * shards : 3 * shards] + total[3 * shards :]
    for r in range(out_ref.shape[0] // shards):
        out_ref[r * shards : (r + 1) * shards, 0, :touch] = count
        out_ref[r * shards : (r + 1) * shards, 0, touch:] = label_sum


def pick_matrix(copies, touched_ref, rows):
    copies.touched.wait()
    touched = touched_ref[...]
    place = lax.broadcasted_iota(jnp.int32, (touched.shape[1], rows), 1)
    return jnp.where(place == to_column(touched), 1.0, 0.0).astype(BF16)


def look_up(copies, picks, table_ref, old_ref):
    copies.table.wait()
    old = jnp.dot(picks, table_ref[...], preferred_element_type=F32).astype(BF16)
    old_ref[...] = old
    return old


def forward(copies, old, w_in_ref, gain_ref):
    copies.w_in.wait()
    pre = jnp.dot(old, w_in_ref[...], preferred_element_type=F32)
    sig_pre = jax.nn.sigmoid(pre)
    hidden = pre * sig_pre
    inv_rms = lax.rsqrt(jnp.mean(hidden * hidden, axis=-1, keepdims=True) + 1e-06)
    copies.gain.wait()
    return pre, sig_pre, hidden, inv_rms


def mix(copies, hidden, inv_rms, gain_ref, w_mid_ref, w_out_ref, stats_ref):
    gain = gain_ref[...]
    normed = (hidden * inv_rms * gain).astype(BF16)
    copies.w_out.wait()
    w_out = w_out_ref[...]
    copies.w_mid.wait()
    features = w_mid_ref.shape[1]
    width = min(features, 256)
    weighted = jnp.zeros((hidden.shape[0], width), F32)
    d_mixed = []
    for start in range(0, features, width):
        part = slice(start, start + width)
        mixed = jnp.dot(normed, w_mid_ref[:, part], preferred_element_type=F32)
        sig_mixed = jax.nn.sigmoid(mixed)
        weighted = weighted + (hidden[:, part] + mixed * sig_mixed) * w_out[:, part]
        d_mixed.append(
            (w_out[:, part] * (sig_mixed * (1.0 + mixed * (1.0 - sig_mixed)))).astype(BF16)
        )
    stats_ref[0:1, :] = jax.nn.sigmoid(to_row(jnp.sum(weighted, axis=-1, keepdims=True)))
    return dot_rows(jnp.concatenate(d_mixed, axis=1), w_mid_ref[...]) * gain


def backward(state, gained, w_in_ref, w_out_ref, grad_ref, stats_ref):
    pre, sig_pre, hidden, inv_rms = state
    d_hidden = (
        w_out_ref[...]
        + inv_rms * gained
        - hidden * inv_rms**3 * jnp.mean(hidden * gained, axis=-1, keepdims=True)
    )
    d_pre = (d_hidden * (sig_pre * (1.0 + pre * (1.0 - sig_pre)))).astype(BF16)
    grad = dot_rows(d_pre, w_in_ref[...])
    grad_ref[...] = grad
    stats_ref[1:2, :] = to_row(jnp.sum(grad * grad, axis=-1, keepdims=True))


def lay_out(copies, touched_ref, spread_ref, acc_ref, stats_ref):
    rows = spread_ref.shape[0]
    touched = touched_ref[...]
    touch = touched.shape[1]
    spread_ref[...] = jnp.where(
        lax.broadcasted_iota(jnp.int32, (rows, touch), 0) == touched, 1.0, 0.0
    ).astype(BF16)
    copies.acc.wait()
    acc = acc_ref[...]
    blocks, lanes = acc.shape
    in_lane = lax.broadcasted_iota(jnp.int32, (lanes, touch), 0) == touched % lanes
    in_block = lax.broadcasted_iota(jnp.int32, (blocks, touch), 0) == touched // lanes
    lane_pick = jnp.where(in_lane, 1.0, 0.0).astype(BF16)
    found = sum(jnp.dot(part, lane_pick, preferred_element_type=F32) for part in split3(acc))
    stats_ref[2:3, :] = jnp.sum(jnp.where(in_block, found, 0.0), axis=0, keepdims=True)
    stats_ref[3:4, :] = touched.astype(F32)


def clear_rows(table_ref, spread_ref, old, base_ref):
    rows = table_ref.shape[0]
    step = min(rows, 256)
    for start in range(0, rows, step):
        part = slice(start, start + step)
        taken = jnp.dot(spread_ref[part, :], old, preferred_element_type=F32).astype(BF16)
        base_ref[part, :] = table_ref[part, :] - taken


def row_gradients(copies, held, weights):
    base_ref, spread_ref, old_ref, grad_ref, stats_ref, acc_ref = held
    touched_ref, w_in_ref, w_mid_ref, gain_ref, w_out_ref = weights
    picks = pick_matrix(copies, touched_ref, base_ref.shape[0])
    lay_out(copies, touched_ref, spread_ref, acc_ref, stats_ref)
    old = look_up(copies, picks, base_ref, old_ref)
    state = forward(copies, old, w_in_ref, gain_ref)
    gained = mix(copies, state[2], state[3], gain_ref, w_mid_ref, w_out_ref, stats_ref)
    backward(state, gained, w_in_ref, w_out_ref, grad_ref, stats_ref)
    clear_rows(base_ref, spread_ref, old, base_ref)


def row_update(got_ref, held, table_hbm, acc_hbm, new_ref, new_acc_ref, sems):
    base_ref, spread_ref, old_ref, grad_ref, stats_ref, acc_ref = held
    rows, touch = spread_ref.shape
    step = new_ref.shape[1]
    parts = rows // step
    summed = jnp.sum(got_ref[...], axis=0)
    d_logit = stats_ref[0:1, :] * summed[:, :touch] - summed[:, touch:]
    acc_new = stats_ref[2:3, :] + d_logit * d_logit * stats_ref[1:2, :]

    factor = jnp.broadcast_to(learn_rate * d_logit * lax.rsqrt(acc_new), (touch, touch)).T
    factor = jnp.concatenate([factor] * (grad_ref.shape[1] // touch), axis=1)
    new_rows = (old_ref[...].astype(F32) - factor * grad_ref[...]).astype(BF16)
    copies = []
    for part in range(parts):
        start = part * step
        moved = jnp.dot(
            spread_ref[start : start + step, :], new_rows, preferred_element_type=F32
        )
        new_ref[part] = base_ref[start : start + step, :] + moved.astype(BF16)
        copy = pltpu.make_async_copy(
            new_ref.at[part], table_hbm.at[pl.ds(start, step), :], sems.at[part]
        )
        copy.start()
        copies.append(copy)

    touched = stats_ref[3:4, :].astype(jnp.int32)
    acc = acc_ref[...]
    blocks, lanes = acc.shape
    in_lane = lax.broadcasted_iota(jnp.int32, (lanes, touch), 0) == touched % lanes
    in_block = lax.broadcasted_iota(jnp.int32, (blocks, touch), 0) == touched // lanes
    lane_pick = jnp.where(in_lane, 1.0, 0.0).astype(BF16)
    block_pick = jnp.where(in_block, 1.0, 0.0).astype(BF16)
    left = jnp.concatenate([block_pick, *split3(jnp.where(in_block, acc_new, 0.0))], axis=0)
    placed = dot_rows(left, lane_pick)
    written = placed[blocks : 2 * blocks] + placed[2 * blocks : 3 * blocks] + placed[3 * blocks :]
    new_acc_ref[...] = jnp.where(placed[:blocks] > 0.5, written, acc)
    copy = pltpu.make_async_copy(new_acc_ref, acc_hbm, sems.at[parts])
    copy.start()
    copies.append(copy)
    for copy in copies:
        copy.wait()


class RowCopies:
    def __init__(self, operands, held, weights, sems):
        touched_hbm, table_hbm, acc_hbm, w_in_hbm, w_mid_hbm, gain_hbm, w_out_hbm = operands
        touched_ref, w_in_ref, w_mid_ref, gain_ref, w_out_ref = weights
        self.small = copies_of(
            [
                (touched_hbm, touched_ref),
                (acc_hbm, held[5]),
                (gain_hbm, gain_ref),
                (w_out_hbm, w_out_ref),
            ],
            sems,
        )
        self.touched, self.acc, self.gain, self.w_out = self.small
        self.table = pltpu.make_async_copy(table_hbm, held[0], sems.at[4])
        self.w_in = pltpu.make_async_copy(w_in_hbm, w_in_ref, sems.at[5])
        self.w_mid = pltpu.make_async_copy(w_mid_hbm, w_mid_ref, sems.at[6])


def before_kernel(shards, *refs):
    event_operands, row_operands = refs[:4], refs[4:11]
    out_ref, held, gained_ref = refs[11], refs[12:18], refs[18]
    event_refs, weights = refs[19:23], refs[23:28]
    event_sems, row_sems = refs[28:]
    near, middle = place_in_mesh()
    not_far = jnp.logical_or(near, middle)
    event_copies = copies_of(zip(event_operands, event_refs), event_sems)
    copies = RowCopies(row_operands, held, weights, row_sems)
    start_all(event_copies)

    @pl.when(not_far)
    def _():
        start_all([*copies.small, copies.table, copies.w_in])

    for copy in event_copies:
        copy.wait()

    @pl.when(not_far)
    def _():
        copies.w_mid.start()

    event_sums(*event_refs, out_ref, shards)

    @pl.when(near)
    def _():
        row_gradients(copies, held, weights)

    @pl.when(middle)
    def _():
        touched_ref, w_in_ref, w_mid_ref, gain_ref, w_out_ref = weights
        picks = pick_matrix(copies, touched_ref, held[0].shape[0])
        old = look_up(copies, picks, held[0], held[2])
        state = forward(copies, old, w_in_ref, gain_ref)
        gained_ref[...] = mix(
            copies, state[2], state[3], gain_ref, w_mid_ref, w_out_ref, held[4]
        )
        copies.acc.wait()


def after_kernel(*refs):
    got_ref, held, gained_ref, row_operands = refs[0], refs[1:7], refs[7], refs[8:15]
    table_hbm, acc_hbm = refs[15:17]
    own_held, weights = refs[17:23], refs[23:28]
    new_ref, new_acc_ref, row_sems, out_sems = refs[28:]
    near, middle = place_in_mesh()
    not_near = jnp.logical_not(near)
    copies = RowCopies(row_operands, own_held, weights, row_sems)

    @pl.when(near)
    def _():
        row_update(got_ref, held, table_hbm, acc_hbm, new_ref, new_acc_ref, out_sems)

    @pl.when(middle)
    def _():
        start_all([*copies.small, copies.w_in])
        table_ref, _, old_ref, _, chances_ref, _ = held
        base_ref, spread_ref, own_old_ref, grad_ref, stats_ref, acc_ref = own_held
        touched_ref, w_in_ref, _, gain_ref, w_out_ref = weights
        old = old_ref[...]
        own_old_ref[...] = old
        stats_ref[0:1, :] = chances_ref[0:1, :]
        copies.touched.wait()
        lay_out(copies, touched_ref, spread_ref, acc_ref, stats_ref)
        clear_rows(table_ref, spread_ref, old, base_ref)
        state = forward(copies, old, w_in_ref, gain_ref)
        copies.w_out.wait()
        backward(state, gained_ref[...], w_in_ref, w_out_ref, grad_ref, stats_ref)

    @pl.when(jnp.logical_and(not_near, jnp.logical_not(middle)))
    def _():
        start_all([*copies.small, copies.table, copies.w_in, copies.w_mid])
        row_gradients(copies, own_held, weights)

    @pl.when(not_near)
    def _():
        row_update(got_ref, own_held, table_hbm, acc_hbm, new_ref, new_acc_ref, out_sems)


def on_device(
    owner_shard,
    slot_index,
    lengths,
    labels,
    embed_table,
    accumulator,
    touched,
    w_in,
    w_mid,
    norm_gain,
    w_out,
):
    shards = lax.axis_size("mp")
    replicas = lax.axis_size("replica")
    rows, width = embed_table.shape
    touch = touched.shape[0]
    lanes = 128

    def stay(array):
        return pltpu.with_memory_space_constraint(array, pltpu.HBM)

    def scratch(array):
        return pltpu.VMEM(array.shape, array.dtype)

    acc = accumulator.reshape(rows // lanes, lanes)
    gain_row = norm_gain.reshape(1, -1)
    w_out_row = w_out.reshape(1, -1)
    touched_row = touched.reshape(1, touch)
    event_operands = (lengths.reshape(1, -1), owner_shard, slot_index, labels)
    row_operands = (touched_row, embed_table, acc, w_in, w_mid, gain_row, w_out_row)
    held_shapes = [
        pltpu.VMEM((rows, width), BF16),
        pltpu.VMEM((rows, touch), BF16),
        pltpu.VMEM((touch, width), BF16),
        pltpu.VMEM((touch, width), F32),
        pltpu.VMEM((8, touch), F32),
        pltpu.VMEM(acc.shape, F32),
    ]
    weight_shapes = [scratch(array) for array in (touched_row, w_in, w_mid, gain_row, w_out_row)]
    memory = pltpu.CompilerParams(vmem_limit_bytes=32 * 1024 * 1024)

    gained_shape = pltpu.VMEM((touch, w_mid.shape[0]), F32)
    sums, *held = pl.pallas_call(
        functools.partial(before_kernel, shards),
        out_shape=(pltpu.VMEM((replicas * shards, 1, 2 * touch), F32), *held_shapes, gained_shape),
        in_specs=[IN_HBM] * 11,
        out_specs=(WHOLE,) * 8,
        scratch_shapes=[
            *[scratch(array) for array in event_operands],
            *weight_shapes,
            pltpu.SemaphoreType.DMA((4,)),
            pltpu.SemaphoreType.DMA((7,)),
        ],
        compiler_params=memory,
        name="before",
    )(*map(stay, event_operands), *map(stay, row_operands))
    got = lax.all_to_all(sums, ("replica", "mp"), 0, 0, tiled=True)

    step = min(rows, 512)
    table_out, acc_out = pl.pallas_call(
        after_kernel,
        out_shape=(pltpu.HBM((rows, width), BF16), pltpu.HBM(acc.shape, F32)),
        in_specs=[WHOLE] * 8 + [IN_HBM] * 7,
        out_specs=(IN_HBM, IN_HBM),
        scratch_shapes=[
            *held_shapes,
            *weight_shapes,
            pltpu.VMEM((rows // step, step, width), BF16),
            pltpu.VMEM(acc.shape, F32),
            pltpu.SemaphoreType.DMA((7,)),
            pltpu.SemaphoreType.DMA((rows // step + 1,)),
        ],
        compiler_params=memory,
        name="after",
    )(got, *held, *map(stay, row_operands))
    return (table_out, acc_out.reshape(rows))


def solution(mesh):
    in_specs = (
        P(("replica", "mp"), None),
        P(("replica", "mp"), None),
        P(("replica", "mp")),
        P(("replica", "mp"), None),
        P("mp", None),
        P("mp"),
        P("mp"),
        P(),
        P(),
        P(),
        P(),
    )
    out_specs = (P("mp", None), P("mp"))
    return jax.shard_map(
        on_device, mesh=mesh, in_specs=in_specs, out_specs=out_specs, check_vma=False
    )
```

time: 18.4 us -> 17.8 us (0.967)
  blocking collectives: 0 us -> 11 us
  starting transfers between devices: 7.3 us -> 0 us
  waiting for transfers between devices: 2.88 us -> 0 us
  Pallas kernels: 7.36 us -> 5.94 us
    all_to_all x0 -> x1, blocking collectives: none -> 11 us  [on_device(): got = lax.all_to_all(sums, ('replica', 'mp'), 0, 0, tiled=True)]
    all_to_all x1 -> x0, starting transfers between devices: 7.3 us -> none  [on_device(): got = lax.all_to_all(sums, ('replica', 'mp'), 0, 0, tiled=True)]
    all_to_all x1 -> x0, waiting for transfers between devices: 2.88 us -> none  [on_device(): got = lax.all_to_all(sums, ('replica', 'mp'), 0, 0, tiled=True)]
    pallas_call x3 -> x2, Pallas kernels: 7.36 us -> 5.94 us  [the longest x1 4.41 us: on_device(): pl.pallas_call(functools.partial(before_kernel, shards), out_shape=(pltpu...]
  transfers between devices with their start and end apart: 1 -> 0, of which waited for: 1 -> 0; matrix products, arithmetic and copies ran while one was open for 0% -> 0% of each run, Pallas kernels for 24% -> 0%
where the time goes in v1:
time: 17.8 us; the launch traced here: 17.6 us
  blocking collectives  11 us (62%)
  Pallas kernels  5.94 us (33%)
  between operations  0.64 us (4%)
    all_to_all x1, blocking collectives, on_device(): got = lax.all_to_all(sums, ('replica', 'mp'), 0, 0, tiled=True)  11 us
    pallas_call x1, Pallas kernels, on_device(): pl.pallas_call(functools.partial(before_kernel, shards), out_shape=(pltpu...  4.41 us
    pallas_call x1, Pallas kernels, on_device(): pl.pallas_call(after_kernel, out_shape=(pltpu.HBM((rows, width), BF16), p...  1.53 us

profile of v1, /device:TPU:0, one launch (start us, length us, event | category | flops | bytes accessed | tf_op | source)
XLA Modules:
  0.0 17.6 jit_solution(10090249447132491200)
XLA Ops:
  0.6 4.4 %before.1 = (f32[32,1,256]{2,1,0:T(1,128)S(1)}, bf16[2048,256]{1,0:T(8,128)(2,1)S(1)}, bf16[2048,128]{1,0:T(8,128)(2,1)S(1)}, bf16[128,256]{1,0:T(8,128)(2,1)S(1...) custom-call(s32[1,2]{1,0:T(1,128)} %bitcast.14, ...), custom_call_target="tpu_custom_call" | custom-call | tf_op jit(solution)/shard_map/before/pallas_call | solution.py:369
  5.1 11.0 %all_to_all.5.refs_0_ = f32[32,1,256]{2,1,0:T(1,128)S(1)} all-to-all(f32[32,1,256]{2,1,0:T(1,128)S(1)} %get-tuple-element.12), channel_id=1, replica_groups=mesh['replica'=2,'mp'=16] {'replica','mp'}, dimensions={0} | all-to-all | bytes 65536 | tf_op jit(solution)/shard_map/all_to_all | solution.py:383
  16.1 1.5 %after.1 = (bf16[2048,256]{1,0:T(8,128)(2,1)}, f32[16,128]{1,0:T(8,128)}) custom-call(f32[32,1,256]{2,1,0:T(1,128)S(1)} %all_to_all.5.refs_0_, bf16[2048,256]{1,0:T(8,128)(2,1)S(1)} %get-tuple-element.13.refs_1_, bf16[2048,128]{1,0:T(8,128)(2,1)S(1)} %get-tuple-element.14.refs_2_, bf16[128,256]{1,0:T(8,128)(2,1)S(1)} %get-tuple-element.15.refs_3_, ...), custom_call_target="tpu_custom_call" | custom-call | tf_op jit(solution)/shard_map/after/pallas_call | solution.py:386

commit v2 on v1

--- a/solution.py
+++ b/solution.py
@@ -61,7 +61,8 @@
     most = replicas - 1 + (places - 1) // 4 + 1
     near = 5 * steps < 2 * most
     middle = jnp.logical_and(jnp.logical_not(near), 2 * steps < most)
-    return near, middle
+    outer = jnp.logical_and(2 * steps >= most, 3 * steps < 2 * most)
+    return near, middle, outer
 
 
 def event_sums(lengths_ref, owner_ref, slot_ref, label_ref, out_ref, shards):
@@ -249,7 +250,7 @@
     out_ref, held, gained_ref = refs[11], refs[12:18], refs[18]
     event_refs, weights = refs[19:23], refs[23:28]
     event_sems, row_sems = refs[28:]
-    near, middle = place_in_mesh()
+    near, middle, outer = place_in_mesh()
     not_far = jnp.logical_or(near, middle)
     event_copies = copies_of(zip(event_operands, event_refs), event_sems)
     copies = RowCopies(row_operands, held, weights, row_sems)
@@ -258,6 +259,10 @@
     @pl.when(not_far)
     def _():
         start_all([*copies.small, copies.table, copies.w_in])
+
+    @pl.when(outer)
+    def _():
+        start_all([copies.touched, copies.table])
 
     for copy in event_copies:
         copy.wait()
@@ -283,14 +288,20 @@
         )
         copies.acc.wait()
 
+    @pl.when(outer)
+    def _():
+        picks = pick_matrix(copies, weights[0], held[0].shape[0])
+        look_up(copies, picks, held[0], held[2])
+
 
 def after_kernel(*refs):
     got_ref, held, gained_ref, row_operands = refs[0], refs[1:7], refs[7], refs[8:15]
     table_hbm, acc_hbm = refs[15:17]
     own_held, weights = refs[17:23], refs[23:28]
     new_ref, new_acc_ref, row_sems, out_sems = refs[28:]
-    near, middle = place_in_mesh()
+    near, middle, outer = place_in_mesh()
     not_near = jnp.logical_not(near)
+    inner = jnp.logical_or(near, middle)
     copies = RowCopies(row_operands, own_held, weights, row_sems)
 
     @pl.when(near)
@@ -313,7 +324,22 @@
         copies.w_out.wait()
         backward(state, gained_ref[...], w_in_ref, w_out_ref, grad_ref, stats_ref)
 
-    @pl.when(jnp.logical_and(not_near, jnp.logical_not(middle)))
+    @pl.when(outer)
+    def _():
+        start_all([*copies.small, copies.w_in, copies.w_mid])
+        table_ref, _, old_ref, _, _, _ = held
+        base_ref, spread_ref, own_old_ref, grad_ref, stats_ref, acc_ref = own_held
+        touched_ref, w_in_ref, w_mid_ref, gain_ref, w_out_ref = weights
+        old = old_ref[...]
+        own_old_ref[...] = old
+        copies.touched.wait()
+        lay_out(copies, touched_ref, spread_ref, acc_ref, stats_ref)
+        clear_rows(table_ref, spread_ref, old, base_ref)
+        state = forward(copies, old, w_in_ref, gain_ref)
+        gained = mix(copies, state[2], state[3], gain_ref, w_mid_ref, w_out_ref, stats_ref)
+        backward(state, gained, w_in_ref, w_out_ref, grad_ref, stats_ref)
+
+    @pl.when(jnp.logical_not(jnp.logical_or(inner, outer)))
     def _():
         start_all([*copies.small, copies.table, copies.w_in, copies.w_mid])
         row_gradients(copies, own_held, weights)
@@ -382,7 +408,7 @@
     )(*map(stay, event_operands), *map(stay, row_operands))
     got = lax.all_to_all(sums, ("replica", "mp"), 0, 0, tiled=True)
 
-    step = min(rows, 512)
+    step = min(rows, 256)
     table_out, acc_out = pl.pallas_call(
         after_kernel,
         out_shape=(pltpu.HBM((rows, width), BF16), pltpu.HBM(acc.shape, F32)),

time: 17.8 us -> 17.7 us (level)
  no operation moved by 1% of the time
where the time goes in v2:
time: 17.7 us; the launch traced here: 17.5 us
  blocking collectives  11 us (62%)
  Pallas kernels  5.87 us (33%)
  between operations  0.64 us (4%)
    all_to_all x1, blocking collectives, on_device(): got = lax.all_to_all(sums, ('replica', 'mp'), 0, 0, tiled=True)  11 us
    pallas_call x1, Pallas kernels, on_device(): pl.pallas_call(functools.partial(before_kernel, shards), out_shape=(pltpu...  4.41 us
    pallas_call x1, Pallas kernels, on_device(): pl.pallas_call(after_kernel, out_shape=(pltpu.HBM((rows, width), BF16), p...  1.46 us

profile of v2, /device:TPU:0, one launch (start us, length us, event | category | flops | bytes accessed | tf_op | source)
XLA Modules:
  0.0 17.5 jit_solution(1514204426748644965)
XLA Ops:
  0.6 4.4 %before.1 = (f32[32,1,256]{2,1,0:T(1,128)S(1)}, bf16[2048,256]{1,0:T(8,128)(2,1)S(1)}, bf16[2048,128]{1,0:T(8,128)(2,1)S(1)}, bf16[128,256]{1,0:T(8,128)(2,1)S(1...) custom-call(s32[1,2]{1,0:T(1,128)} %bitcast.14, ...), custom_call_target="tpu_custom_call" | custom-call | tf_op jit(solution)/shard_map/before/pallas_call | solution.py:395
  5.1 11.0 %all_to_all.5.refs_0_ = f32[32,1,256]{2,1,0:T(1,128)S(1)} all-to-all(f32[32,1,256]{2,1,0:T(1,128)S(1)} %get-tuple-element.12), channel_id=1, replica_groups=mesh['replica'=2,'mp'=16] {'replica','mp'}, dimensions={0} | all-to-all | bytes 65536 | tf_op jit(solution)/shard_map/all_to_all | solution.py:409
  16.1 1.5 %after.1 = (bf16[2048,256]{1,0:T(8,128)(2,1)}, f32[16,128]{1,0:T(8,128)}) custom-call(f32[32,1,256]{2,1,0:T(1,128)S(1)} %all_to_all.5.refs_0_, bf16[2048,256]{1,0:T(8,128)(2,1)S(1)} %get-tuple-element.13.refs_1_, bf16[2048,128]{1,0:T(8,128)(2,1)S(1)} %get-tuple-element.14.refs_2_, bf16[128,256]{1,0:T(8,128)(2,1)S(1)} %get-tuple-element.15.refs_3_, ...), custom_call_target="tpu_custom_call" | custom-call | tf_op jit(solution)/shard_map/after/pallas_call | solution.py:412

commit v3 on v1

--- a/solution.py
+++ b/solution.py
@@ -67,16 +67,17 @@
 def event_sums(lengths_ref, owner_ref, slot_ref, label_ref, out_ref, shards):
     samples, length = owner_ref.shape
     touch = out_ref.shape[2] // 2
-    total = jnp.zeros((4 * shards, touch), F32)
+    place = lax.broadcasted_iota(jnp.int32, (shards, length), 1)
+    shard = lax.broadcasted_iota(jnp.int32, (shards, length), 0)
+    slot = lax.broadcasted_iota(jnp.int32, (touch, length), 0)
+    lefts, rights = [], []
     for s in range(samples):
-        place = lax.broadcasted_iota(jnp.int32, (shards, length), 1)
-        shard = lax.broadcasted_iota(jnp.int32, (shards, length), 0)
         chosen = (owner_ref[s : s + 1, :] == shard) & (place < lengths_ref[:, s : s + 1])
-        slot = lax.broadcasted_iota(jnp.int32, (touch, length), 0)
-        slots = jnp.where(slot_ref[s : s + 1, :] == slot, 1.0, 0.0).astype(BF16)
-        labels = jnp.where(chosen, label_ref[s : s + 1, :], 0.0)
-        left = jnp.concatenate([jnp.where(chosen, 1.0, 0.0).astype(BF16), *split3(labels)], axis=0)
-        total = total + dot_rows(left, slots)
+        picked = jnp.where(chosen, 1.0, 0.0).astype(BF16)
+        parts = [part * picked for part in split3(label_ref[s : s + 1, :])]
+        lefts.append(jnp.concatenate([picked, *parts], axis=0))
+        rights.append(jnp.where(slot_ref[s : s + 1, :] == slot, 1.0, 0.0).astype(BF16))
+    total = dot_rows(jnp.concatenate(lefts, axis=1), jnp.concatenate(rights, axis=1))
     count = total[:shards]
     label_sum = total[shards : 2 * shards] + total[2 * shards : 3 * shards] + total[3 * shards :]
     for r in range(out_ref.shape[0] // shards):
@@ -382,7 +383,7 @@
     )(*map(stay, event_operands), *map(stay, row_operands))
     got = lax.all_to_all(sums, ("replica", "mp"), 0, 0, tiled=True)
 
-    step = min(rows, 512)
+    step = min(rows, 256)
     table_out, acc_out = pl.pallas_call(
         after_kernel,
         out_shape=(pltpu.HBM((rows, width), BF16), pltpu.HBM(acc.shape, F32)),

time: 17.8 us -> 17.7 us (level)
  no operation moved by 1% of the time
where the time goes in v3:
time: 17.7 us; the launch traced here: 17.5 us
  blocking collectives  11 us (62%)
  Pallas kernels  5.88 us (33%)
  between operations  0.64 us (4%)
    all_to_all x1, blocking collectives, on_device(): got = lax.all_to_all(sums, ('replica', 'mp'), 0, 0, tiled=True)  11 us
    pallas_call x1, Pallas kernels, on_device(): pl.pallas_call(functools.partial(before_kernel, shards), out_shape=(pltpu...  4.41 us
    pallas_call x1, Pallas kernels, on_device(): pl.pallas_call(after_kernel, out_shape=(pltpu.HBM((rows, width), BF16), p...  1.46 us

profile of v3, /device:TPU:0, one launch (start us, length us, event | category | flops | bytes accessed | tf_op | source)
XLA Modules:
  0.0 17.5 jit_solution(16206653357698701782)
XLA Ops:
  0.6 4.4 %before.1 = (f32[32,1,256]{2,1,0:T(1,128)S(1)}, bf16[2048,256]{1,0:T(8,128)(2,1)S(1)}, bf16[2048,128]{1,0:T(8,128)(2,1)S(1)}, bf16[128,256]{1,0:T(8,128)(2,1)S(1...) custom-call(s32[1,2]{1,0:T(1,128)} %bitcast.14, ...), custom_call_target="tpu_custom_call" | custom-call | tf_op jit(solution)/shard_map/before/pallas_call | solution.py:370
  5.1 11.0 %all_to_all.5.refs_0_ = f32[32,1,256]{2,1,0:T(1,128)S(1)} all-to-all(f32[32,1,256]{2,1,0:T(1,128)S(1)} %get-tuple-element.12), channel_id=1, replica_groups=mesh['replica'=2,'mp'=16] {'replica','mp'}, dimensions={0} | all-to-all | bytes 65536 | tf_op jit(solution)/shard_map/all_to_all | solution.py:384
  16.1 1.5 %after.1 = (bf16[2048,256]{1,0:T(8,128)(2,1)}, f32[16,128]{1,0:T(8,128)}) custom-call(f32[32,1,256]{2,1,0:T(1,128)S(1)} %all_to_all.5.refs_0_, bf16[2048,256]{1,0:T(8,128)(2,1)S(1)} %get-tuple-element.13.refs_1_, bf16[2048,128]{1,0:T(8,128)(2,1)S(1)} %get-tuple-element.14.refs_2_, bf16[128,256]{1,0:T(8,128)(2,1)S(1)} %get-tuple-element.15.refs_3_, ...), custom_call_target="tpu_custom_call" | custom-call | tf_op jit(solution)/shard_map/after/pallas_call | solution.py:387
